TPU v7x, 128 devices: a whole 4x4x4 slice. The times are simulated.
128 devices in a mesh: dp: 16 (over z, x_lo, core), tensor: 8 (over y, x_hi).
Axes of the slice: x: 4 (x_hi: 2, x_lo: 2; x = x_hi * 2 + x_lo), y: 4, z: 4, core: 2. Of those that a mesh axis runs over, the one named last changes fastest.
Arguments:
- lm_grad: bfloat16 [8192, 3200], P(('dp', 'tensor')), may hold values from -6 to 6
- encoder_row: int32 [8192], P(('dp', 'tensor')), may hold values from 0 to 8191, as said below
- patch_count: int32 [16], replicated, may hold values from 256 to 512, as said below
- hidden_in: bfloat16 [8192, 3200], P(('dp', 'tensor'))
- norm_gain: float32 [3200], replicated, may hold values from 0.5 to 2
- layer_scale: float32 [3200], replicated, may hold values from 0.3 to 3
- up_weight: bfloat16 [3200, 12800], P(None, 'tensor'), may hold values from -0.109375 to 0.109375
- down_weight: bfloat16 [3200, 12800], P(None, 'tensor'), may hold values from -0.0546875 to 0.0546875
Outputs:
- input_grad: bfloat16 [8192, 3200], P(('dp', 'tensor'))
- up_grad: bfloat16 [3200, 12800], P('dp', 'tensor')
- down_grad: bfloat16 [3200, 12800], P('dp', 'tensor')
Inputs may be any that keep to these rules, and one draw needn't show every extreme that they name: `encoder_row`: A permutation of the 8192 encoder rows. The 64 rows of one device hold exactly 4 rows of each image. `patch_count`: in every draw some image is full.
All inputs are finite; a program needn't handle non-finite values.
Results may differ from a plain program's by a relative error of at most 0.024.
Values may be sent and summed in bfloat16 or wider, within the bound.
No kernel may reach another device: no remote copies, remote signals or barrier semaphores. Data moves between devices by JAX's collectives and lax.ppermute only.
A program may use at most 192 MiB of HBM per device.

v0:
```python
import math

import jax
import jax.numpy as jnp
from jax import lax
from jax.sharding import PartitionSpec as P


def gelu_slope(value):
    return (
        0.5 * (1.0 + lax.erf(value * 0.7071067811865476))
        + value * jnp.exp(-0.5 * value * value) * 0.3989422804014327
    )


def column_term(left_side, right_side):
    return lax.dot_general(
        left_side, right_side, (((0,), (0,)), ((), ())), preferred_element_type=jnp.float32
    )


def on_device(
    lm_grad, encoder_row, patch_count, hidden_in, norm_gain, layer_scale, up_weight, down_weight
):
    tp_size = lax.axis_size("tensor")
    dp_size = lax.axis_size("dp")
    tok_rows = hidden_in.shape[0]
    width = hidden_in.shape[1]
    group_len = tok_rows * tp_size
    group = lax.axis_index("dp")
    member = lax.axis_index("tensor")
    joined, joined_ids = (
        lax.all_gather(lm_grad, "tensor", axis=0, tiled=True),
        lax.all_gather(encoder_row, "tensor", axis=0, tiled=True),
    )
    sorter = jnp.argsort(joined_ids // group_len, stable=True)
    arrived, arrived_ids = (
        lax.all_to_all(joined[sorter], "dp", split_axis=0, concat_axis=0, tiled=True),
        lax.all_to_all(joined_ids[sorter], "dp", split_axis=0, concat_axis=0, tiled=True),
    )
    grad_group = (
        jnp.zeros((group_len, width), jnp.bfloat16).at[arrived_ids % group_len].set(arrived)
    )
    positions = jnp.arange(group_len, dtype=jnp.int32)
    limit = lax.dynamic_index_in_dim(patch_count, group, 0, keepdims=False)
    valid = (positions < limit)[:, None]
    scaled_grad = jnp.where(valid, layer_scale * grad_group.astype(jnp.float32), 0.0).astype(
        jnp.bfloat16
    )
    own_grad = lax.dynamic_slice_in_dim(grad_group, member * tok_rows, tok_rows, 0).astype(
        jnp.float32
    )
    own_valid = lax.dynamic_slice_in_dim(valid, member * tok_rows, tok_rows, 0)
    inputs = hidden_in.astype(jnp.float32)
    inverse_rms = lax.rsqrt(jnp.mean(inputs * inputs, -1, keepdims=True) + 1e-06)
    normed_own = (inputs * inverse_rms * norm_gain).astype(jnp.bfloat16)
    normed = lax.all_gather(normed_own, "tensor", axis=0, tiled=True)
    pre_act = jnp.dot(normed, up_weight, preferred_element_type=jnp.float32)
    activation = jax.nn.gelu(pre_act, approximate=False).astype(jnp.bfloat16)
    act_grad = jnp.dot(scaled_grad, down_weight, preferred_element_type=jnp.float32)
    pre_grad = (act_grad * gelu_slope(pre_act)).astype(jnp.bfloat16)
    normed_grad = lax.psum_scatter(
        lax.dot_general(
            pre_grad, up_weight, (((1,), (1,)), ((), ())), preferred_element_type=jnp.float32
        ).astype(jnp.bfloat16),
        "tensor",
        scatter_dimension=0,
        tiled=True,
    ).astype(jnp.float32)
    weighted = norm_gain * normed_grad
    input_grad = (
        jnp.where(own_valid, own_grad, 0.0)
        + inverse_rms * weighted
        - inputs * inverse_rms**3 * jnp.mean(weighted * inputs, -1, keepdims=True)
    ).astype(jnp.bfloat16)
    up_sum = lax.psum_scatter(
        column_term(normed, pre_grad).astype(jnp.bfloat16), "dp", scatter_dimension=0, tiled=True
    ).astype(jnp.float32)
    down_sum = lax.psum_scatter(
        column_term(scaled_grad, activation).astype(jnp.bfloat16),
        "dp",
        scatter_dimension=0,
        tiled=True,
    ).astype(jnp.float32)
    grad_scale = 1.0 / math.sqrt(group_len * dp_size)
    return (
        input_grad,
        (up_sum * grad_scale).astype(jnp.bfloat16),
        (down_sum * grad_scale).astype(jnp.bfloat16),
    )


def solution(mesh):
    in_specs = (
        P(("dp", "tensor"), None),
        P(("dp", "tensor")),
        P(),
        P(("dp", "tensor"), None),
        P(),
        P(),
        P(None, "tensor"),
        P(None, "tensor"),
    )
    out_specs = (P(("dp", "tensor"), None), P("dp", "tensor"), P("dp", "tensor"))
    return jax.shard_map(
        on_device, mesh=mesh, in_specs=in_specs, out_specs=out_specs, check_vma=False
    )
```

profile of v0, /device:TPU:24, one launch (start us, length us, event | category | flops | bytes accessed | tf_op | source)
XLA Modules:
  0.0 536.2 jit_solution(6201786182390558989)
XLA Ops:
  7.2 0.7 all-gather.3.cloned.1.call-update
  7.9 1.2 fusion.48
  9.1 1.9 fusion.50
  11.1 1.2 dynamic-slice.4
  13.0 0.9 dynamic-update-slice
  13.9 10.7 %all-reduce = s32[512]{0:T(512)S(1)} all-reduce(s32[512]{0:T(512)S(1)} %dynamic-update-slice), channel_id=1, replica_groups=mesh['dp'=16,'tensor'=8] {'tensor'}, use_global_device_ids=true, to_apply=%add | all-reduce | flops 512 | bytes 4096
  24.5 3.8 sort.17
  28.3 3.5 gather_fusion
  31.8 0.7 all_to_all.16
  32.5 6.4 %all-to-all-start = ((s32[16,32,1]{1,2,0:T(1,128)}), s32[16,32,1]{1,2,0:T(1,128)S(1)}, u32[]{:S(2)}, u32[]{:S(2)}) async-start(s32[16,32,1]{1,2,0:T(1,128)} %bitcast.2), calls=%async_computation | async-start | bytes 16384 | tf_op jit(solution)/shard_map/all_to_all | solution.py:39
  38.9 35.3 %all-gather.3.cloned.1.call-done = bf16[512,3200]{1,0:T(8,128)(2,1)} async-done(((bf16[64,3200]{1,0:T(8,128)(2,1)}), bf16[512,3200]{1,0:T(8,128)(2,1)}) %all-gather.3.cloned.1.call-update) | async-done | bytes 3276816 | tf_op jit(solution)/shard_map/all_gather | solution.py:33
  74.2 9.6 %gather_fusion.1 = bf16[512,3200]{1,0:T(8,128)(2,1)} fusion(bf16[512,3200]{1,0:T(8,128)(2,1)} %all-gather.3.cloned.1.call-done, s32[1024]{0:T(1024)S(1)} %pad_clamp_fusion), kind=kCustom, calls=%fused_computation.1 | custom fusion | bytes 6555648 | tf_op jit(solution)/shard_map/gather | solution.py:38
  83.9 4.7 all-to-all-start.1
  89.4 0.6 iota_compare_fusion
  90.5 0.7 reduce.3
  91.3 65.1 %all-gather.5.cloned.1.call-done = bf16[512,3200]{1,0:T(8,128)(2,1)} async-done(((bf16[64,3200]{1,0:T(8,128)(2,1)}), bf16[512,3200]{1,0:T(8,128)(2,1)}) %all-gather.5.cloned.1.call-update) | async-done | bytes 3276816 | tf_op jit(solution)/shard_map/all_gather | solution.py:57
  156.4 11.7 %fusion.89 = f32[512,1600]{0,1:T(8,128)} fusion(bf16[512,3200]{1,0:T(8,128)(2,1)} %all-gather.5.cloned.1.call-done, bf16[3200,1600]{0,1:T(8,128)(2,1)} %param.14), kind=kOutput, calls=%fused_computation.128 | convolution fusion | flops 5242880000 | bytes 16793600 | tf_op jit(solution)/shard_map/dot_general | solution.py:58
  168.1 1.7 copy-done.2
  169.8 7.6 %scatter_custom_fusion = bf16[512,3200]{1,0:T(8,128)(2,1)S(1)} fusion(s32[512]{0:T(512)S(1)} %bitcast.17, bf16[512,3200]{1,0:T(8,128)(2,1)} %bitcast.16, bf16[]{:T(256)} %constant.27.clone.1), kind=kCustom, calls=%fused_computation.63 | custom fusion | bytes 3277312 | tf_op jit(solution)/shard_map/scatter | solution.py:42
  177.4 12.6 %fusion.14 = bf16[512,1600]{0,1:T(8,128)(2,1)S(1)} fusion(f32[512,1600]{0,1:T(8,128)} %fusion.89, bf16[3200,1600]{0,1:T(8,128)(2,1)} %param.15, bf16[512,3200]{1,0:T(8,128)(2,1)S(1)} %scatter_custom_fusion, f32[3200]{0:T(1024)S(1)} %copy-done.5, pred[512]{0:T(512)(128)(4,1)S(1)} %iota_compare_fusion), kind=kOutput, calls=%fused_computation.32 | convolution fusion | flops 5257625600 | bytes 18445312 | tf_op jit(solution)/shard_map/dot_general | solution.py:60
  190.0 1.2 copy-done.7
  191.2 11.7 %convolution_convert_fusion.2 = bf16[512,3200]{1,0:T(8,128)(2,1)} fusion(bf16[512,1600]{0,1:T(8,128)(2,1)S(1)} %fusion.14, bf16[3200,1600]{0,1:T(8,128)(2,1)} %param.14), kind=kOutput, calls=%fused_computation.6 | convolution fusion | flops 5244518400 | bytes 15155200 | tf_op jit(solution)/shard_map/dot_general | solution.py:63
  203.2 17.2 %convolution_convert_fusion = bf16[3200,1600]{1,0:T(8,128)(2,1)} fusion(f32[512,1600]{0,1:T(8,128)} %fusion.89, bf16[512,3200]{1,0:T(8,128)(2,1)S(1)} %scatter_custom_fusion, f32[3200]{0:T(1024)S(1)} %copy-done.5, pred[512]{0:T(512)(128)(4,1)S(1)} %iota_compare_fusion), kind=kOutput, calls=%fused_computation.3 | convolution fusion | flops 5307801600 | bytes 16806912 | tf_op jit(solution)/shard_map/dot_general | solution.py:17
  220.5 1.9 copy-done.4
  222.4 10.3 %convolution_convert_fusion.1 = bf16[3200,1600]{1,0:T(8,128)(2,1)} fusion(bf16[512,3200]{1,0:T(8,128)(2,1)S(1)} %copy-done.4, bf16[512,1600]{0,1:T(8,128)(2,1)} %copy-done.7), kind=kOutput, calls=%fused_computation.4 | convolution fusion | flops 5248000000 | bytes 15155200 | tf_op jit(solution)/shard_map/dot_general | solution.py:17
  232.9 49.2 %reduce-scatter.10.cloned.1.call-done = bf16[64,3200]{1,0:T(8,128)(2,1)} async-done(((bf16[512,3200]{1,0:T(8,128)(2,1)}), bf16[64,3200]{1,0:T(8,128)(2,1)}) %reduce-scatter.10.cloned.1.call-update) | async-done | bytes 409616 | tf_op jit(solution)/shard_map/reduce_scatter | solution.py:62
  282.1 1.2 fusion.54
  283.4 2.2 fusion.53
  285.6 119.6 %reduce-scatter.14.cloned.1.call-done = bf16[200,1600]{1,0:T(8,128)(2,1)} async-done(((bf16[3200,1600]{1,0:T(8,128)(2,1)}), bf16[200,1600]{1,0:T(8,128)(2,1)}) %reduce-scatter.14.cloned.1.call-update) | async-done | bytes 640016
  405.1 2.0 multiply_convert_fusion
  407.2 120.4 %reduce-scatter.12.cloned.1.call-done = bf16[200,1600]{1,0:T(8,128)(2,1)} async-done(((bf16[3200,1600]{1,0:T(8,128)(2,1)}), bf16[200,1600]{1,0:T(8,128)(2,1)}) %reduce-scatter.12.cloned.1.call-update) | async-done | bytes 640016
  527.6 2.0 multiply_convert_fusion.1
  (36 shorter events, 2.0 us)
Async XLA Ops:
  7.2 67.1 %all-gather.3.cloned.1.call-start = ((), (), s32[]{:S(2)}) async-start(), calls=%async_computation.5 | async-start | bytes 3686400 | tf_op jit(solution)/shard_map/all_gather | solution.py:33
  7.9 148.5 %all-gather.5.cloned.1.call-start = ((), (), s32[]{:S(2)}) async-start(), calls=%async_computation.6 | async-start | bytes 3686400 | tf_op jit(solution)/shard_map/all_gather | solution.py:57
  32.5 51.4 %all-to-all-start = ((s32[16,32,1]{1,2,0:T(1,128)}), s32[16,32,1]{1,2,0:T(1,128)S(1)}, u32[]{:S(2)}, u32[]{:S(2)}) async-start(s32[16,32,1]{1,2,0:T(1,128)} %bitcast.2), calls=%async_computation | async-start | bytes 16384 | tf_op jit(solution)/shard_map/all_to_all | solution.py:39
  83.9 4.9 copy-start.6
  83.9 84.3 %all-to-all-start.1 = ((bf16[16,32,3200]{2,1,0:T(8,128)(2,1)}), bf16[16,32,3200]{2,1,0:T(8,128)(2,1)S(1)}, u32[]{:S(2)}, u32[]{:S(2)}) async-start(bf16[16,32,3200]{2,1,0:T(8,128)(2,1)} %bitcast.4), calls=%async_computation.1 | async-start | bytes 6553600 | tf_op jit(solution)/shard_map/all_to_all | solution.py:38
  88.5 193.6 %reduce-scatter.10.cloned.1.call-start = ((), (), s32[]{:S(2)}) async-start(), calls=%async_computation.7 | async-start | bytes 3686400 | tf_op jit(solution)/shard_map/reduce_scatter | solution.py:62
  168.1 9.3 %copy-start.5 = (f32[3200]{0:T(1024)S(1)}, f32[3200]{0:T(1024)}, u32[]{:S(2)}) copy-start(f32[3200]{0:T(1024)} %param.13) | copy-start | bytes 38404
  168.1 1.7 copy-start.2
  177.4 25.8 %copy-start.1 = (bf16[512,3200]{1,0:T(8,128)(2,1)}, bf16[512,3200]{1,0:T(8,128)(2,1)S(1)}, u32[]{:S(2)}) copy-start(bf16[512,3200]{1,0:T(8,128)(2,1)S(1)} %scatter_custom_fusion) | copy-start | bytes 9830404
  190.0 1.2 copy-start.7
  202.9 202.2 %reduce-scatter.14.cloned.1.call-start = ((), (), s32[]{:S(2)}) async-start(), calls=%async_computation.9 | async-start | bytes 11315200
  220.4 2.0 copy-start.4
  220.5 307.1 %reduce-scatter.12.cloned.1.call-start = ((), (), s32[]{:S(2)}) async-start(), calls=%async_computation.8 | async-start | bytes 11315200
  232.8 49.3 %copy-start = (bf16[64,3200]{1,0:T(8,128)(2,1)S(1)}, bf16[64,3200]{1,0:T(8,128)(2,1)}, u32[]{:S(2)}) copy-start(bf16[64,3200]{1,0:T(8,128)(2,1)} %param.11) | copy-start | bytes 1228804
  232.8 49.3 %copy-start.3 = (f32[3200]{0:T(1024)S(1)}, f32[3200]{0:T(1024)}, u32[]{:S(2)}) copy-start(f32[3200]{0:T(1024)} %param.12) | copy-start | bytes 38404
Sparse Core Ops, SparseCore 0:
  10.3 63.8 all-gather.2
  77.1 79.2 all-gather.4
  203.1 79.0 reduce-scatter.9
  284.5 120.5 reduce-scatter.13
  407.5 120.0 reduce-scatter.11
where the time goes:
time: 537 us; the launch traced here: 536 us
  waiting for transfers between devices  390 us (73%)
  matrix products  63.5 us (12%)
  local copies, waits for them, and re-layouts  29.6 us (6%)
  other arithmetic  15.8 us (3%)
  between operations  14.6 us (3%)
  starting transfers between devices  11.7 us (2%)
  blocking collectives  10.7 us (2%)
    unnamed x7, waiting for transfers between devices  241 us
    all_gather x1, waiting for transfers between devices, on_device(): normed = lax.all_gather(normed_own, 'tensor', axis=0, tiled=True)  65.1 us
    reduce_scatter x1, waiting for transfers between devices, on_device(): lax.psum_scatter(lax.dot_general(pre_grad, up_weight, (((1,), (1,)), ((),...  49.2 us
    all_gather x1, waiting for transfers between devices, on_device(): lax.all_gather(lm_grad, 'tensor', axis=0, tiled=True)  35.3 us
    dot_general x2, matrix products, column_term(): lax.dot_general(left_side, right_side, (((0,), (0,)), ((), ())), preferre...  27.5 us
    dot_general x1, matrix products, on_device(): jnp.dot(scaled_grad, down_weight, preferred_element_type=jnp.float32)  12.6 us
    dot_general x1, matrix products, on_device(): lax.dot_general(pre_grad, up_weight, (((1,), (1,)), ((), ())), preferred_...  11.7 us
    dot_general x1, matrix products, on_device(): pre_act = jnp.dot(normed, up_weight, preferred_element_type=jnp.float32)  11.7 us
  transfers between devices with their start and end apart: 7, of which 5 were waited for; matrix products, arithmetic and copies ran while one was open for 13% of the time, Pallas kernels for 0%

commit v1 on v0

v1 whole, which is shorter than its diff:
```python
import math

import jax
import jax.numpy as jnp
from jax import lax
from jax.sharding import Mesh, PartitionSpec as P

F32 = jnp.float32
BF16 = jnp.bfloat16
Z, XL, CORE, Y, XH = 4, 2, 2, 4, 2
AXES = ("z", "xl", "core", "y", "xh")
ID_COLS = 128
ID_BASE = 32


def gelu_slope(value):
    return (
        0.5 * (1.0 + lax.erf(value * 0.7071067811865476))
        + value * jnp.exp(-0.5 * value * value) * 0.3989422804014327
    )


def shift(value, axis, size, step):
    return lax.ppermute(value, axis, [(i, (i + step) % size) for i in range(size)])


def add(*terms):
    total = terms[0].astype(F32)
    for term in terms[1:]:
        total = total + term.astype(F32)
    return total.astype(BF16)


def column_term(left_side, right_side):
    return lax.dot_general(
        left_side, right_side, (((0,), (0,)), ((), ())), preferred_element_type=F32
    ).astype(BF16)


def gather_rows(own):
    half = own.shape[0] // 2
    from_prev = shift(own, "y", Y, 1)
    from_next = shift(own, "y", Y, -1)
    other = shift(own, "xh", XH, 1)
    far = jnp.concatenate(
        [shift(from_prev[:half], "y", Y, 1), shift(from_next[half:], "y", Y, -1)], 0
    )
    other_prev = shift(other, "y", Y, 1)
    other_next = shift(other, "y", Y, -1)
    other_far = shift(far, "xh", XH, 1)
    return jnp.concatenate(
        [own, other, from_next, other_next, far, other_far, from_prev, other_prev], 0
    )


def scatter_rows(parts):
    rows = parts.shape[0] // 8
    half = rows // 2
    own, other, nxt, other_nxt, far, other_far, prev, other_prev = (
        parts[i * rows : (i + 1) * rows] for i in range(8)
    )
    got_far = shift(other_far, "xh", XH, 1)
    got_other_prev = shift(other_nxt, "y", Y, 1)
    got_other_next = shift(other_prev, "y", Y, -1)
    far = add(far, got_far)
    pass_prev = shift(far[:half], "y", Y, 1)
    pass_next = shift(far[half:], "y", Y, -1)
    got_other = shift(add(other, got_other_prev, got_other_next), "xh", XH, 1)
    nxt = jnp.concatenate([add(nxt[:half], pass_prev), nxt[half:]], 0)
    prev = jnp.concatenate([prev[:half], add(prev[half:], pass_next)], 0)
    got_prev = shift(nxt, "y", Y, 1)
    got_next = shift(prev, "y", Y, -1)
    return own.astype(F32) + got_prev.astype(F32) + got_next.astype(F32) + got_other.astype(F32)


def add_cores(grad):
    core = lax.axis_index("core")
    rows = grad.shape[0] // (Z * XL * CORE)
    view = grad.reshape(Z, XL, CORE, rows, grad.shape[1])
    give = lax.dynamic_index_in_dim(view, 1 - core, 2, keepdims=False)
    keep = lax.dynamic_index_in_dim(view, core, 2, keepdims=False)
    return add(keep, shift(give, "core", CORE, 1))


def z_first(grad):
    z, xl = lax.axis_index("z"), lax.axis_index("xl")
    total = add_cores(grad)

    def part(dz, x):
        return lax.dynamic_index_in_dim(total, (z + dz) % Z, 0, keepdims=False)[x]

    from_prev = shift(jnp.stack([part(2, 0), part(1, 1)]), "z", Z, 1)
    from_next = shift(jnp.stack([part(2, 1), part(3, 0)]), "z", Z, -1)
    acc_prev = shift(add(part(1, 0), from_prev[0]), "z", Z, 1)
    acc_next = shift(add(part(3, 1), from_next[0]), "z", Z, -1)
    sums = (
        add(part(0, 0), from_next[1], acc_prev),
        add(part(0, 1), from_prev[1], acc_next),
    )
    give = jnp.where(xl == 0, sums[1], sums[0])
    keep = jnp.where(xl == 0, sums[0], sums[1])
    return keep.astype(F32) + shift(give, "xl", XL, 1).astype(F32)


def x_first(grad):
    z, xl = lax.axis_index("z"), lax.axis_index("xl")
    total = add_cores(grad)
    rows = total.shape[2]
    cut = -(-rows // 16) * 8

    def part(dz, x):
        both = lax.dynamic_index_in_dim(total, (z + dz) % Z, 0, keepdims=False)
        return lax.dynamic_index_in_dim(both, x, 0, keepdims=False)

    early = shift(jnp.stack([part(2, 1 - xl), part(1, 1 - xl)]), "xl", XL, 1)
    late = shift(jnp.stack([part(3, 1 - xl), part(0, 1 - xl)]), "xl", XL, 1)
    two = add(part(2, xl), early[0])
    one = add(part(1, xl), early[1])
    three = add(part(3, xl), late[0])
    here = part(0, xl).astype(F32) + late[1].astype(F32)
    from_prev = shift(jnp.concatenate([two[:cut], one[cut:]], 0), "z", Z, 1)
    from_next = shift(jnp.concatenate([three[:cut], two[cut:]], 0), "z", Z, -1)
    acc_prev = shift(add(one[:cut], from_prev[:cut]), "z", Z, 1)
    acc_next = shift(add(three[cut:], from_next[cut:]), "z", Z, -1)
    return jnp.concatenate(
        [
            here[:cut] + from_next[:cut].astype(F32) + acc_prev.astype(F32),
            here[cut:] + from_prev[cut:].astype(F32) + acc_next.astype(F32),
        ],
        0,
    )


def on_device(
    lm_grad, encoder_row, patch_count, hidden_in, norm_gain, layer_scale, up_weight, down_weight
):
    tok_rows, width = hidden_in.shape
    members = Y * XH
    groups = Z * XL * CORE
    group_len = tok_rows * members
    per_pair = tok_rows // groups
    z, xl, core = lax.axis_index("z"), lax.axis_index("xl"), lax.axis_index("core")
    y, xh = lax.axis_index("y"), lax.axis_index("xh")
    group = (z * XL + xl) * CORE + core

    inputs = hidden_in.astype(F32)
    inverse_rms = lax.rsqrt(jnp.mean(inputs * inputs, -1, keepdims=True) + 1e-06)
    normed_own = (inputs * inverse_rms * norm_gain).astype(BF16)

    image, place = encoder_row // group_len, encoder_row % group_len
    index = jnp.arange(tok_rows, dtype=jnp.int32)
    same = (image[:, None] == image[None, :]) & (index[None, :] < index[:, None])
    slot = image * per_pair + jnp.sum(same.astype(jnp.int32), 1)
    sorter = (slot[None, :] == index[:, None]).astype(BF16)
    column = jnp.arange(ID_COLS, dtype=jnp.int32)[None, :]
    tags = jnp.where(
        column == 0,
        (place // ID_BASE)[:, None],
        jnp.where(column == 1, (place % ID_BASE)[:, None], 0),
    ).astype(BF16)
    rows = jnp.concatenate([lm_grad, tags], 1)
    ordered = jnp.dot(sorter, rows, preferred_element_type=F32).astype(BF16)
    arrived = lax.all_to_all(
        ordered.reshape(groups, per_pair, width + ID_COLS),
        ("z", "xl", "core"),
        split_axis=0,
        concat_axis=0,
    ).reshape(tok_rows, width + ID_COLS)

    normed = gather_rows(normed_own)
    joined = gather_rows(arrived)

    block = jnp.arange(members, dtype=jnp.int32)
    member = ((block // XH + y) % Y) * XH + (block % XH + xh) % XH
    positions = (member[:, None] * tok_rows + index[None, :]).reshape(group_len)
    limit = lax.dynamic_index_in_dim(patch_count, group, 0, keepdims=False)
    places = (
        joined[:, width].astype(jnp.int32) * ID_BASE + joined[:, width + 1].astype(jnp.int32)
    )
    chooser = (
        (positions[:, None] == places[None, :]) & (positions < limit)[:, None]
    ).astype(BF16)
    grads = jnp.dot(chooser, joined[:, :width], preferred_element_type=F32)
    scaled_grad = (grads * layer_scale).astype(BF16)
    own_grad = jnp.dot(chooser[:tok_rows], joined[:, :width], preferred_element_type=F32)

    pre_act = jnp.dot(normed, up_weight, preferred_element_type=F32)
    activation = jax.nn.gelu(pre_act, approximate=False).astype(BF16)
    slope = gelu_slope(pre_act)
    cut = 896
    down_a = z_first(column_term(scaled_grad, activation[:, :cut]))
    down_b = x_first(column_term(scaled_grad, activation[:, cut:]))
    act_grad = jnp.dot(scaled_grad, down_weight, preferred_element_type=F32)
    pre_grad = (act_grad * slope).astype(BF16)
    up_a = z_first(column_term(normed, pre_grad[:, :cut]))
    up_b = x_first(column_term(normed, pre_grad[:, cut:]))

    normed_grad = scatter_rows(
        lax.dot_general(
            pre_grad, up_weight, (((1,), (1,)), ((), ())), preferred_element_type=F32
        ).astype(BF16)
    )
    weighted = norm_gain * normed_grad
    input_grad = (
        own_grad
        + inverse_rms * weighted
        - inputs * inverse_rms**3 * jnp.mean(weighted * inputs, -1, keepdims=True)
    ).astype(BF16)
    grad_scale = 1.0 / math.sqrt(group_len * groups)
    return (
        input_grad,
        (jnp.concatenate([up_a, up_b], 1) * grad_scale).astype(BF16),
        (jnp.concatenate([down_a, down_b], 1) * grad_scale).astype(BF16),
    )


def solution(mesh):
    fine = Mesh(mesh.devices.reshape(Z, XL, CORE, Y, XH), AXES)
    dp, tensor = ("z", "xl", "core"), ("y", "xh")
    in_specs = (
        P(AXES, None),
        P(AXES),
        P(),
        P(AXES, None),
        P(),
        P(),
        P(None, tensor),
        P(None, tensor),
    )
    out_specs = (P(AXES, None), P(dp, tensor), P(dp, tensor))
    return jax.shard_map(
        on_device, mesh=fine, in_specs=in_specs, out_specs=out_specs, check_vma=False
    )
```

time: 537 us -> 345 us (0.64)
  waiting for transfers between devices: 390 us -> 149 us
  starting transfers between devices: 11.7 us -> 74.8 us
  between operations: 14.6 us -> 1.99 us
  blocking collectives: 10.7 us -> 0 us
  other arithmetic: 15.8 us -> 22.8 us
  matrix products: 63.5 us -> 58.1 us
    unnamed x7 -> x0, waiting for transfers between devices: 241 us -> none
    ppermute x0 -> x50, waiting for transfers between devices: none -> 140 us  [shift(): lax.ppermute(value, axis, [(i, (i + step) % size) for i in range(size)])]
    all_gather x2 -> x0, waiting for transfers between devices: 100 us -> none  [the longest x1 65.1 us: on_device(): normed = lax.all_gather(normed_own, 'tensor', axis=0, tiled=True)]
    ppermute x0 -> x50, starting transfers between devices: none -> 69.4 us  [shift(): lax.ppermute(value, axis, [(i, (i + step) % size) for i in range(size)])]
    reduce_scatter x1 -> x0, waiting for transfers between devices: 49.2 us -> none  [on_device(): lax.psum_scatter(lax.dot_general(pre_grad, up_weight, (((1,), (1,)), ((),...]
    convert_element_type x0 -> x2, local copies, waits for them, and re-layouts: none -> 15 us  [column_term(): return lax.dot_general(left_side, right_side, (((0,), (0,)), ((), ())), p...]
    gather x2 -> x0, local copies, waits for them, and re-layouts: 13.1 us -> none  [the longest x1 9.63 us: on_device(): joined[sorter]]
    unnamed x1 -> x0, blocking collectives: 10.7 us -> none
  transfers between devices with their start and end apart: 7 -> 51, of which waited for: 5 -> 24; matrix products, arithmetic and copies ran while one was open for 13% -> 19% of each run, Pallas kernels for 0% -> 0%
where the time goes in v1:
time: 345 us; the launch traced here: 339 us
  waiting for transfers between devices  149 us (43%)
  starting transfers between devices  74.8 us (22%)
  matrix products  58.1 us (17%)
  local copies, waits for them, and re-layouts  32.6 us (9%)
  other arithmetic  22.8 us (7%)
    ppermute x50, waiting for transfers between devices, shift(): lax.ppermute(value, axis, [(i, (i + step) % size) for i in range(size)])  140 us
    ppermute x50, starting transfers between devices, shift(): lax.ppermute(value, axis, [(i, (i + step) % size) for i in range(size)])  69.4 us
    dot_general x4, matrix products, column_term(): lax.dot_general(left_side, right_side, (((0,), (0,)), ((), ())), preferre...  21.5 us
    dot_general x1, matrix products, on_device(): pre_act = jnp.dot(normed, up_weight, preferred_element_type=F32)  16.7 us
    convert_element_type x2, local copies, waits for them, and re-layouts, column_term(): return lax.dot_general(left_side, right_side, (((0,), (0,)), ((), ())), p...  15 us
    convert_element_type x14, other arithmetic, add(): return total.astype(BF16)  12.5 us
    unnamed x59, local copies, waits for them, and re-layouts  8.77 us
    all_to_all x1, waiting for transfers between devices, on_device(): lax.all_to_all(ordered.reshape(groups, per_pair, width + ID_COLS), ('z',...  8.33 us
  transfers between devices with their start and end apart: 51, of which 24 were waited for; matrix products, arithmetic and copies ran while one was open for 19% of the time, Pallas kernels for 0%

profile of v1, /device:TPU:24, one launch (start us, length us, event | category | flops | bytes accessed | tf_op | source)
XLA Modules:
  0.0 339.1 jit_solution(172117189114692388)
XLA Ops:
  13.2 5.4 %all-to-all-start = ((bf16[16,4,3328]{2,1,0:T(4,128)(2,1)}), bf16[16,4,3328]{2,1,0:T(4,128)(2,1)S(1)}, u32[]{:S(2)}, u32[]{:S(2)}) async-start(bf16[16,4,3328]{2,1,0:T(4,128)(2,1)} %reshape.268), calls=%async_computation | async-start | bytes 851968 | tf_op jit(solution)/shard_map/all_to_all | solution.py:163
  20.1 8.3 %all-to-all-done = bf16[16,4,3328]{2,1,0:T(4,128)(2,1)S(1)} async-done(((bf16[16,4,3328]{2,1,0:T(4,128)(2,1)}), bf16[16,4,3328]{2,1,0:T(4,128)(2,1)S(1)}, u32[]{:S(2)}, u32[]{:S(2)}) %all-to-all-start) | async-done | bytes 426016 | tf_op jit(solution)/shard_map/all_to_all | solution.py:163
  30.7 3.3 collective-permute-start.3
  37.8 8.6 %collective-permute-done.12 = bf16[32,3200]{1,0:T(8,128)(2,1)S(1)} collective-permute-done((bf16[32,3200]{1,0:T(8,128)(2,1)S(1)}, bf16[32,3200]{1,0:T(8,128)(2,1)S(1)}, u32[]{:S(2)}, u32[]{:S(2)}) %collective-permute-start.12) | collective-permute-done | bytes 204832 | tf_op jit(solution)/shard_map/ppermute | solution.py:24
  50.1 7.4 %collective-permute-done.10 = bf16[64,3200]{1,0:T(8,128)(2,1)S(1)} collective-permute-done((bf16[64,3200]{1,0:T(8,128)(2,1)S(1)}, bf16[64,3200]{1,0:T(8,128)(2,1)S(1)}, u32[]{:S(2)}, u32[]{:S(2)}) %collective-permute-start.10) | collective-permute-done | bytes 409632 | tf_op jit(solution)/shard_map/ppermute | solution.py:24
  63.6 4.0 %collective-permute-done.14 = bf16[64,3200]{1,0:T(8,128)(2,1)S(1)} collective-permute-done((bf16[64,3200]{1,0:T(8,128)(2,1)S(1)}, bf16[64,3200]{1,0:T(8,128)(2,1)S(1)}, u32[]{:S(2)}, u32[]{:S(2)}) %collective-permute-start.14) | collective-permute-done | bytes 409632 | tf_op jit(solution)/shard_map/ppermute | solution.py:24
  77.1 5.6 %collective-permute-done.6 = bf16[64,3328]{1,0:T(8,128)(2,1)S(1)} collective-permute-done((bf16[64,3328]{1,0:T(8,128)(2,1)S(1)}, bf16[64,3328]{1,0:T(8,128)(2,1)S(1)}, u32[]{:S(2)}, u32[]{:S(2)}) %collective-permute-start.6) | collective-permute-done | bytes 426016 | tf_op jit(solution)/shard_map/ppermute | solution.py:24
  86.6 7.6 %fusion.80 = f32[512,1600]{0,1:T(8,128)} fusion(bf16[512,3200]{1,0:T(8,128)(2,1)S(1)} %fusion, bf16[3200,1600]{0,1:T(8,128)(2,1)S(1)} %bitcast.236), kind=kOutput, calls=%fused_computation.249 | convolution fusion | flops 5242880000 | bytes 16793600 | tf_op jit(solution)/shard_map/dot_general | solution.py:193
  94.3 16.7 %fusion.15 = (bf16[512,1600]{0,1:T(8,128)(2,1)}, bf16[512,1600]{0,1:T(8,128)(2,1)S(1)}) fusion(f32[512,1600]{0,1:T(8,128)} %fusion.80, bf16[512,3200]{1,0:T(8,128)(2,1)S(1)} %copy-done.7, bf16[3200,1600]{0,1:T(8,128)(2,1)S(1)} %bitcast.238), kind=kOutput, calls=%fused_computation.29 | convolution fusion | flops 5304320000 | bytes 20070400 | tf_op jit(solution)/shard_map/dot_general | solution.py:187
  111.0 6.7 %convolution_convert_fusion.4 = bf16[512,3200]{1,0:T(8,128)(2,1)S(1)} fusion(bf16[512,1600]{0,1:T(8,128)(2,1)S(1)} %get-tuple-element.16, bf16[3200,1600]{0,1:T(8,128)(2,1)S(1)} %bitcast.238), kind=kOutput, calls=%fused_computation.6 | convolution fusion | flops 5244518400 | bytes 15155200 | tf_op jit(solution)/shard_map/dot_general | solution.py:199
  119.5 4.2 %convolution_convert_fusion.3 = bf16[3200,704]{0,1:T(8,128)(2,1)} fusion(bf16[512,3200]{1,0:T(8,128)(2,1)S(1)} %copy-done.7, bf16[512,1600]{0,1:T(8,128)(2,1)S(1)} %get-tuple-element.16), kind=kOutput, calls=%fused_computation.4 | convolution fusion | flops 2309120000 | bytes 8503296 | tf_op jit(solution)/shard_map/dot_general | solution.py:35
  123.7 5.5 %convolution_convert_fusion.1 = bf16[3200,896]{1,0:T(8,128)(2,1)} fusion(bf16[512,3200]{1,0:T(8,128)(2,1)S(1)} %copy-done.7, bf16[512,1600]{0,1:T(8,128)(2,1)S(1)} %get-tuple-element.16), kind=kOutput, calls=%fused_computation.1 | convolution fusion | flops 2938880000 | bytes 9928704 | tf_op jit(solution)/shard_map/dot_general | solution.py:35
  131.3 3.2 collective-permute-start.21
  134.5 7.3 %copy.27 = bf16[3200,704]{1,0:T(8,128)(2,1)} copy(bf16[3200,704]{0,1:T(8,128)(2,1)} %convolution_convert_fusion.3) | data formatting | bytes 9011200 | tf_op jit(solution)/shard_map/convert_element_type | solution.py:37
  141.8 3.4 %dynamic-slice_bitcast_fusion.3 = bf16[4,2,200,704]{3,2,1,0:T(8,128)(2,1)} fusion(bf16[4,2,2,200,704]{4,3,2,1,0:T(8,128)(2,1)} %bitcast.225, s32[]{:T(128)S(6)} %select_n.262), kind=kLoop, calls=%fused_computation.50 | loop fusion | bytes 4505604 | tf_op jit(solution)/shard_map/jit(dynamic_index_in_dim)/squeeze | solution.py:80
  145.3 5.8 %convolution_convert_fusion.2 = bf16[3200,704]{0,1:T(8,128)(2,1)} fusion(bf16[512,3200]{1,0:T(8,128)(2,1)S(1)} %copy-done.11, bf16[512,1600]{0,1:T(8,128)(2,1)} %get-tuple-element.15), kind=kOutput, calls=%fused_computation.3 | convolution fusion | flops 2309120000 | bytes 8503296 | tf_op jit(solution)/shard_map/dot_general | solution.py:35
  151.1 7.6 %copy.29 = bf16[3200,704]{1,0:T(8,128)(2,1)} copy(bf16[3200,704]{0,1:T(8,128)(2,1)} %convolution_convert_fusion.2) | data formatting | bytes 9011200 | tf_op jit(solution)/shard_map/convert_element_type | solution.py:37
  158.7 5.9 %convolution_convert_fusion = bf16[3200,896]{1,0:T(8,128)(2,1)S(1)} fusion(bf16[512,3200]{1,0:T(8,128)(2,1)} %copy-done.10, bf16[512,1600]{0,1:T(8,128)(2,1)} %get-tuple-element.15), kind=kOutput, calls=%fused_computation | convolution fusion | flops 2938880000 | bytes 9928704 | tf_op jit(solution)/shard_map/dot_general | solution.py:35
  170.5 3.3 collective-permute-done.17
  182.3 5.3 %collective-permute-done.20 = bf16[64,3200]{1,0:T(8,128)(2,1)S(1)} collective-permute-done((bf16[64,3200]{1,0:T(8,128)(2,1)S(1)}, bf16[64,3200]{1,0:T(8,128)(2,1)S(1)}, u32[]{:S(2)}, u32[]{:S(2)}) %collective-permute-start.20) | collective-permute-done | bytes 409632 | tf_op jit(solution)/shard_map/ppermute | solution.py:24
  197.3 10.1 %collective-permute-done.32 = bf16[2,200,704]{2,1,0:T(8,128)(2,1)S(1)} collective-permute-done((bf16[2,200,704]{2,1,0:T(8,128)(2,1)S(1)}, bf16[2,200,704]{2,1,0:T(8,128)(2,1)S(1)}, u32[]{:S(2)}, u32[]{:S(2)}) %collective-permute-start.32) | collective-permute-done | bytes 563232 | tf_op jit(solution)/shard_map/ppermute | solution.py:24
  211.8 8.8 %collective-permute-done.31 = bf16[2,200,704]{2,1,0:T(8,128)(2,1)S(1)} collective-permute-done((bf16[2,200,704]{2,1,0:T(8,128)(2,1)S(1)}, bf16[2,200,704]{2,1,0:T(8,128)(2,1)S(1)}, u32[]{:S(2)}, u32[]{:S(2)}) %collective-permute-start.31) | collective-permute-done | bytes 563232 | tf_op jit(solution)/shard_map/ppermute | solution.py:24
  220.9 12.8 %collective-permute-done.45 = bf16[2,200,704]{2,1,0:T(8,128)(2,1)S(1)} collective-permute-done((bf16[2,200,704]{2,1,0:T(8,128)(2,1)S(1)}, bf16[2,200,704]{2,1,0:T(8,128)(2,1)S(1)}, u32[]{:S(2)}, u32[]{:S(2)}) %collective-permute-start.45) | collective-permute-done | bytes 563232 | tf_op jit(solution)/shard_map/ppermute | solution.py:24
  233.7 12.9 %collective-permute-done.44 = bf16[2,200,704]{2,1,0:T(8,128)(2,1)S(1)} collective-permute-done((bf16[2,200,704]{2,1,0:T(8,128)(2,1)S(1)}, bf16[2,200,704]{2,1,0:T(8,128)(2,1)S(1)}, u32[]{:S(2)}, u32[]{:S(2)}) %collective-permute-start.44) | collective-permute-done | bytes 563232 | tf_op jit(solution)/shard_map/ppermute | solution.py:24
  260.8 3.3 collective-permute-start.38
  269.4 28.0 %collective-permute-done.36 = bf16[96,704]{1,0:T(8,128)(2,1)S(1)} collective-permute-done((bf16[96,704]{1,0:T(8,128)(2,1)S(1)}, bf16[96,704]{1,0:T(8,128)(2,1)S(1)}, u32[]{:S(2)}, u32[]{:S(2)}) %collective-permute-start.36) | collective-permute-done | bytes 135200 | tf_op jit(solution)/shard_map/ppermute | solution.py:24
  298.7 4.0 %collective-permute-done.49 = bf16[96,704]{1,0:T(8,128)(2,1)S(1)} collective-permute-done((bf16[96,704]{1,0:T(8,128)(2,1)S(1)}, bf16[96,704]{1,0:T(8,128)(2,1)S(1)}, u32[]{:S(2)}, u32[]{:S(2)}) %collective-permute-start.49) | collective-permute-done | bytes 135200 | tf_op jit(solution)/shard_map/ppermute | solution.py:24
  306.9 4.1 %collective-permute-done.35 = bf16[104,704]{1,0:T(8,128)(2,1)S(1)} collective-permute-done((bf16[104,704]{1,0:T(8,128)(2,1)S(1)}, bf16[104,704]{1,0:T(8,128)(2,1)S(1)}, u32[]{:S(2)}, u32[]{:S(2)}) %collective-permute-start.35) | collective-permute-done | bytes 146464 | tf_op jit(solution)/shard_map/ppermute | solution.py:24
  315.7 6.4 %collective-permute-done.27 = bf16[200,896]{1,0:T(8,128)(2,1)S(1)} collective-permute-done((bf16[200,896]{1,0:T(8,128)(2,1)S(1)}, bf16[200,896]{1,0:T(8,128)(2,1)S(1)}, u32[]{:S(2)}, u32[]{:S(2)}) %collective-permute-start.27) | collective-permute-done | bytes 358432 | tf_op jit(solution)/shard_map/ppermute | solution.py:24
  323.8 3.5 %collective-permute-done.40 = bf16[200,896]{1,0:T(8,128)(2,1)S(1)} collective-permute-done((bf16[200,896]{1,0:T(8,128)(2,1)S(1)}, bf16[200,896]{1,0:T(8,128)(2,1)S(1)}, u32[]{:S(2)}, u32[]{:S(2)}) %collective-permute-start.40) | collective-permute-done | bytes 358432 | tf_op jit(solution)/shard_map/ppermute | solution.py:24
  328.5 3.1 collective-permute-done.29
  332.7 4.8 %collective-permute-done.42 = bf16[200,896]{1,0:T(8,128)(2,1)S(1)} collective-permute-done((bf16[200,896]{1,0:T(8,128)(2,1)S(1)}, bf16[200,896]{1,0:T(8,128)(2,1)S(1)}, u32[]{:S(2)}, u32[]{:S(2)}) %collective-permute-start.42) | collective-permute-done | bytes 358432 | tf_op jit(solution)/shard_map/ppermute | solution.py:24
  (230 shorter events, 109.8 us)
Async XLA Ops:
  3.8 30.3 %collective-permute-start.8 = (bf16[64,3200]{1,0:T(8,128)(2,1)S(1)}, bf16[64,3200]{1,0:T(8,128)(2,1)S(1)}, u32[]{:S(2)}, u32[]{:S(2)}) collective-permute-start(bf16[64,3200]{1,0:T(8,128)(2,1)S(1)} %get-tuple-element.10), channel_id=1, source_target_pairs={{0,1},{1,0},{2,3},{3,2},{4,5},{5,4},{6,7},{7,6},{8,9},{9,8},{10,11... | collective-permute-start | bytes 1228808 | tf_op jit(solution)/shard_map/ppermute | solution.py:24
  6.8 27.1 %collective-permute-start.9 = (bf16[64,3200]{1,0:T(8,128)(2,1)S(1)}, bf16[64,3200]{1,0:T(8,128)(2,1)S(1)}, u32[]{:S(2)}, u32[]{:S(2)}) collective-permute-start(bf16[64,3200]{1,0:T(8,128)(2,1)S(1)} %get-tuple-element.10), channel_id=1, source_target_pairs={{0,6},{2,0},{4,2},{6,4},{1,7},{3,1},{5,3},{7,5},{8,14},{10,8},{12,... | collective-permute-start | bytes 1228808 | tf_op jit(solution)/shard_map/ppermute | solution.py:24
  7.6 23.1 %collective-permute-start.11 = (bf16[64,3200]{1,0:T(8,128)(2,1)S(1)}, bf16[64,3200]{1,0:T(8,128)(2,1)S(1)}, u32[]{:S(2)}, u32[]{:S(2)}) collective-permute-start(bf16[64,3200]{1,0:T(8,128)(2,1)S(1)} %get-tuple-element.10), channel_id=1, source_target_pairs={{0,2},{2,4},{4,6},{6,0},{1,3},{3,5},{5,7},{7,1},{8,10},{10,12},{12... | collective-permute-start | bytes 1228808 | tf_op jit(solution)/shard_map/ppermute | solution.py:24
  13.2 15.3 %all-to-all-start = ((bf16[16,4,3328]{2,1,0:T(4,128)(2,1)}), bf16[16,4,3328]{2,1,0:T(4,128)(2,1)S(1)}, u32[]{:S(2)}, u32[]{:S(2)}) async-start(bf16[16,4,3328]{2,1,0:T(4,128)(2,1)} %reshape.268), calls=%async_computation | async-start | bytes 851968 | tf_op jit(solution)/shard_map/all_to_all | solution.py:163
  28.5 34.9 %collective-permute-start = (bf16[64,3328]{1,0:T(8,128)(2,1)S(1)}, bf16[64,3328]{1,0:T(8,128)(2,1)S(1)}, u32[]{:S(2)}, u32[]{:S(2)}) collective-permute-start(bf16[64,3328]{1,0:T(8,128)(2,1)S(1)} %reshape.269), channel_id=1, source_target_pairs={{0,1},{1,0},{2,3},{3,2},{4,5},{5,4},{6,7},{7,6},{8,9},{9,8},{10,11... | collective-permute-start | bytes 1277960 | tf_op jit(solution)/shard_map/ppermute | solution.py:24
  30.6 32.5 %collective-permute-start.1 = (bf16[64,3328]{1,0:T(8,128)(2,1)S(1)}, bf16[64,3328]{1,0:T(8,128)(2,1)S(1)}, u32[]{:S(2)}, u32[]{:S(2)}) collective-permute-start(bf16[64,3328]{1,0:T(8,128)(2,1)S(1)} %reshape.269), channel_id=1, source_target_pairs={{0,6},{2,0},{4,2},{6,4},{1,7},{3,1},{5,3},{7,5},{8,14},{10,8},{12,... | collective-permute-start | bytes 1277960 | tf_op jit(solution)/shard_map/ppermute | solution.py:24
  30.7 30.6 %collective-permute-start.3 = (bf16[64,3328]{1,0:T(8,128)(2,1)S(1)}, bf16[64,3328]{1,0:T(8,128)(2,1)S(1)}, u32[]{:S(2)}, u32[]{:S(2)}) collective-permute-start(bf16[64,3328]{1,0:T(8,128)(2,1)S(1)} %reshape.269), channel_id=1, source_target_pairs={{0,2},{2,4},{4,6},{6,0},{1,3},{3,5},{5,7},{7,1},{8,10},{10,12},{12... | collective-permute-start | bytes 1277960 | tf_op jit(solution)/shard_map/ppermute | solution.py:24
  47.0 23.7 %collective-permute-start.15 = (bf16[64,3200]{1,0:T(8,128)(2,1)S(1)}, bf16[64,3200]{1,0:T(8,128)(2,1)S(1)}, u32[]{:S(2)}, u32[]{:S(2)}) collective-permute-start(bf16[64,3200]{1,0:T(8,128)(2,1)S(1)} %collective-permute-done.8), channel_id=1, source_target_pairs={{0,2},{2,4},{4,6},{6,0},{1,3},{3,5},{5,7},{7,1},{8,10},{10,12},{12... | collective-permute-start | bytes 1228808 | tf_op jit(solution)/shard_map/ppermute | solution.py:24
  67.7 15.1 %collective-permute-start.7 = (bf16[64,3328]{1,0:T(8,128)(2,1)S(1)}, bf16[64,3328]{1,0:T(8,128)(2,1)S(1)}, u32[]{:S(2)}, u32[]{:S(2)}) collective-permute-start(bf16[64,3328]{1,0:T(8,128)(2,1)S(1)} %collective-permute-done), channel_id=1, source_target_pairs={{0,2},{2,4},{4,6},{6,0},{1,3},{3,5},{5,7},{7,1},{8,10},{10,12},{12... | collective-permute-start | bytes 1277960 | tf_op jit(solution)/shard_map/ppermute | solution.py:24
  129.2 35.4 %collective-permute-start.16 = (bf16[64,3200]{1,0:T(8,128)(2,1)S(1)}, bf16[64,3200]{1,0:T(8,128)(2,1)}, u32[]{:S(2)}, u32[]{:S(2)}) collective-permute-start(bf16[64,3200]{1,0:T(8,128)(2,1)S(1)} %get-tuple-element.23), channel_id=1, source_target_pairs={{0,1},{1,0},{2,3},{3,2},{4,5},{5,4},{6,7},{7,6},{8,9},{9,8},{10,11... | collective-permute-start | bytes 1228808 | tf_op jit(solution)/shard_map/ppermute | solution.py:24
  131.3 33.4 %collective-permute-start.22 = (bf16[64,3200]{1,0:T(8,128)(2,1)S(1)}, bf16[64,3200]{1,0:T(8,128)(2,1)}, u32[]{:S(2)}, u32[]{:S(2)}) collective-permute-start(bf16[64,3200]{1,0:T(8,128)(2,1)S(1)} %get-tuple-element.24), channel_id=1, source_target_pairs={{0,6},{2,0},{4,2},{6,4},{1,7},{3,1},{5,3},{7,5},{8,14},{10,8},{12,... | collective-permute-start | bytes 1228808 | tf_op jit(solution)/shard_map/ppermute | solution.py:24
  131.3 33.4 %collective-permute-start.21 = (bf16[64,3200]{1,0:T(8,128)(2,1)S(1)}, bf16[64,3200]{1,0:T(8,128)(2,1)}, u32[]{:S(2)}, u32[]{:S(2)}) collective-permute-start(bf16[64,3200]{1,0:T(8,128)(2,1)S(1)} %get-tuple-element.25), channel_id=1, source_target_pairs={{0,2},{2,4},{4,6},{6,0},{1,3},{3,5},{5,7},{7,1},{8,10},{10,12},{12... | collective-permute-start | bytes 1228808 | tf_op jit(solution)/shard_map/ppermute | solution.py:24
  145.3 42.8 %collective-permute-start.30 = (bf16[4,2,200,704]{3,2,1,0:T(8,128)(2,1)}, bf16[4,2,200,704]{3,2,1,0:T(8,128)(2,1)}, u32[]{:S(2)}, u32[]{:S(2)}) collective-permute-start(bf16[4,2,200,704]{3,2,1,0:T(8,128)(2,1)} %dynamic-slice_bitcast_fusion.3), channel_id=1, source_target_pairs={{0,8},{8,0},{1,9},{9,1},{2,10},{10,2},{3,11},{11,3},{4,12},{12,4},... | collective-permute-start | bytes 6758408 | tf_op jit(solution)/shard_map/ppermute | solution.py:24
  168.5 24.3 %collective-permute-start.43 = (bf16[4,2,200,704]{3,2,1,0:T(8,128)(2,1)S(1)}, bf16[4,2,200,704]{3,2,1,0:T(8,128)(2,1)}, u32[]{:S(2)}, u32[]{:S(2)}) collective-permute-start(bf16[4,2,200,704]{3,2,1,0:T(8,128)(2,1)S(1)} %dynamic-slice_bitcast_fusion.2), channel_id=1, source_target_pairs={{0,8},{8,0},{1,9},{9,1},{2,10},{10,2},{3,11},{11,3},{4,12},{12,4},... | collective-permute-start | bytes 6758408 | tf_op jit(solution)/shard_map/ppermute | solution.py:24
  182.3 69.2 %collective-permute-start.24 = (bf16[4,2,200,896]{3,2,1,0:T(8,128)(2,1)S(1)}, bf16[4,2,200,896]{3,2,1,0:T(8,128)(2,1)}, u32[]{:S(2)}, u32[]{:S(2)}) collective-permute-start(bf16[4,2,200,896]{3,2,1,0:T(8,128)(2,1)S(1)} %dynamic-slice_bitcast_fusion.1), channel_id=1, source_target_pairs={{0,8},{8,0},{1,9},{9,1},{2,10},{10,2},{3,11},{11,3},{4,12},{12,4},... | collective-permute-start | bytes 8601608 | tf_op jit(solution)/shard_map/ppermute | solution.py:24
  187.6 67.0 %collective-permute-start.37 = (bf16[4,2,200,896]{3,2,1,0:T(8,128)(2,1)}, bf16[4,2,200,896]{3,2,1,0:T(8,128)(2,1)}, u32[]{:S(2)}, u32[]{:S(2)}) collective-permute-start(bf16[4,2,200,896]{3,2,1,0:T(8,128)(2,1)} %dynamic-slice_bitcast_fusion), channel_id=1, source_target_pairs={{0,8},{8,0},{1,9},{9,1},{2,10},{10,2},{3,11},{11,3},{4,12},{12,4},... | collective-permute-start | bytes 8601608 | tf_op jit(solution)/shard_map/ppermute | solution.py:24
  190.6 16.8 %collective-permute-start.32 = (bf16[2,200,704]{2,1,0:T(8,128)(2,1)S(1)}, bf16[2,200,704]{2,1,0:T(8,128)(2,1)S(1)}, u32[]{:S(2)}, u32[]{:S(2)}) collective-permute-start(bf16[2,200,704]{2,1,0:T(8,128)(2,1)S(1)} %pad_maximum_fusion.5), channel_id=1, source_target_pairs={{0,16},{16,0},{1,17},{17,1},{2,18},{18,2},{3,19},{19,3},{4,20},{20... | collective-permute-start | bytes 1689608 | tf_op jit(solution)/shard_map/ppermute | solution.py:24
  192.6 28.0 %collective-permute-start.31 = (bf16[2,200,704]{2,1,0:T(8,128)(2,1)S(1)}, bf16[2,200,704]{2,1,0:T(8,128)(2,1)S(1)}, u32[]{:S(2)}, u32[]{:S(2)}) collective-permute-start(bf16[2,200,704]{2,1,0:T(8,128)(2,1)S(1)} %pad_maximum_fusion.4), channel_id=1, source_target_pairs={{0,16},{16,0},{1,17},{17,1},{2,18},{18,2},{3,19},{19,3},{4,20},{20... | collective-permute-start | bytes 1689608 | tf_op jit(solution)/shard_map/ppermute | solution.py:24
  195.3 38.4 %collective-permute-start.45 = (bf16[2,200,704]{2,1,0:T(8,128)(2,1)S(1)}, bf16[2,200,704]{2,1,0:T(8,128)(2,1)S(1)}, u32[]{:S(2)}, u32[]{:S(2)}) collective-permute-start(bf16[2,200,704]{2,1,0:T(8,128)(2,1)S(1)} %pad_maximum_fusion.7), channel_id=1, source_target_pairs={{0,16},{16,0},{1,17},{17,1},{2,18},{18,2},{3,19},{19,3},{4,20},{20... | collective-permute-start | bytes 1689608 | tf_op jit(solution)/shard_map/ppermute | solution.py:24
  207.4 39.2 %collective-permute-start.44 = (bf16[2,200,704]{2,1,0:T(8,128)(2,1)S(1)}, bf16[2,200,704]{2,1,0:T(8,128)(2,1)S(1)}, u32[]{:S(2)}, u32[]{:S(2)}) collective-permute-start(bf16[2,200,704]{2,1,0:T(8,128)(2,1)S(1)} %pad_maximum_fusion.6), channel_id=1, source_target_pairs={{0,16},{16,0},{1,17},{17,1},{2,18},{18,2},{3,19},{19,3},{4,20},{20... | collective-permute-start | bytes 1689608 | tf_op jit(solution)/shard_map/ppermute | solution.py:24
  247.1 13.7 %collective-permute-start.33 = (bf16[200,704]{1,0:T(8,128)(2,1)S(1)}, bf16[200,704]{1,0:T(8,128)(2,1)S(1)}, u32[]{:S(2)}, u32[]{:S(2)}) collective-permute-start(bf16[200,704]{1,0:T(8,128)(2,1)S(1)} %pad_maximum_fusion.12), channel_id=1, source_target_pairs={{0,96},{32,0},{64,32},{96,64},{1,97},{33,1},{65,33},{97,65},{2,98}... | collective-permute-start | bytes 844808 | tf_op jit(solution)/shard_map/ppermute | solution.py:24
  249.6 16.7 %collective-permute-start.46 = (bf16[200,704]{1,0:T(8,128)(2,1)S(1)}, bf16[200,704]{1,0:T(8,128)(2,1)S(1)}, u32[]{:S(2)}, u32[]{:S(2)}) collective-permute-start(bf16[200,704]{1,0:T(8,128)(2,1)S(1)} %pad_maximum_fusion.14), channel_id=1, source_target_pairs={{0,96},{32,0},{64,32},{96,64},{1,97},{33,1},{65,33},{97,65},{2,98}... | collective-permute-start | bytes 844808 | tf_op jit(solution)/shard_map/ppermute | solution.py:24
  251.5 14.5 %collective-permute-start.47 = (bf16[200,704]{1,0:T(8,128)(2,1)S(1)}, bf16[200,704]{1,0:T(8,128)(2,1)S(1)}, u32[]{:S(2)}, u32[]{:S(2)}) collective-permute-start(bf16[200,704]{1,0:T(8,128)(2,1)S(1)} %pad_maximum_fusion.15), channel_id=1, source_target_pairs={{0,32},{32,64},{64,96},{96,0},{1,33},{33,65},{65,97},{97,1},{2,34}... | collective-permute-start | bytes 844808 | tf_op jit(solution)/shard_map/ppermute | solution.py:24
  254.6 49.7 %collective-permute-start.25 = (bf16[2,200,896]{2,1,0:T(8,128)(2,1)S(1)}, bf16[2,200,896]{2,1,0:T(8,128)(2,1)S(1)}, u32[]{:S(2)}, u32[]{:S(2)}) collective-permute-start(bf16[2,200,896]{2,1,0:T(8,128)(2,1)S(1)} %pad_maximum_fusion), channel_id=1, source_target_pairs={{0,96},{32,0},{64,32},{96,64},{1,97},{33,1},{65,33},{97,65},{2,98}... | collective-permute-start | bytes 2150408 | tf_op jit(solution)/shard_map/ppermute | solution.py:24
  260.6 43.8 %collective-permute-start.26 = (bf16[2,200,896]{2,1,0:T(8,128)(2,1)S(1)}, bf16[2,200,896]{2,1,0:T(8,128)(2,1)S(1)}, u32[]{:S(2)}, u32[]{:S(2)}) collective-permute-start(bf16[2,200,896]{2,1,0:T(8,128)(2,1)S(1)} %pad_maximum_fusion.1), channel_id=1, source_target_pairs={{0,32},{32,64},{64,96},{96,0},{1,33},{33,65},{65,97},{97,1},{2,34}... | collective-permute-start | bytes 2150408 | tf_op jit(solution)/shard_map/ppermute | solution.py:24
  260.8 51.4 %collective-permute-start.38 = (bf16[2,200,896]{2,1,0:T(8,128)(2,1)S(1)}, bf16[2,200,896]{2,1,0:T(8,128)(2,1)S(1)}, u32[]{:S(2)}, u32[]{:S(2)}) collective-permute-start(bf16[2,200,896]{2,1,0:T(8,128)(2,1)S(1)} %pad_maximum_fusion.2), channel_id=1, source_target_pairs={{0,96},{32,0},{64,32},{96,64},{1,97},{33,1},{65,33},{97,65},{2,98}... | collective-permute-start | bytes 2150408 | tf_op jit(solution)/shard_map/ppermute | solution.py:24
  266.0 46.1 %collective-permute-start.39 = (bf16[2,200,896]{2,1,0:T(8,128)(2,1)S(1)}, bf16[2,200,896]{2,1,0:T(8,128)(2,1)S(1)}, u32[]{:S(2)}, u32[]{:S(2)}) collective-permute-start(bf16[2,200,896]{2,1,0:T(8,128)(2,1)S(1)} %pad_maximum_fusion.3), channel_id=1, source_target_pairs={{0,32},{32,64},{64,96},{96,0},{1,33},{33,65},{65,97},{97,1},{2,34}... | collective-permute-start | bytes 2150408 | tf_op jit(solution)/shard_map/ppermute | solution.py:24
  266.3 31.1 %collective-permute-start.36 = (bf16[96,704]{1,0:T(8,128)(2,1)S(1)}, bf16[96,704]{1,0:T(8,128)(2,1)S(1)}, u32[]{:S(2)}, u32[]{:S(2)}) collective-permute-start(bf16[96,704]{1,0:T(8,128)(2,1)S(1)} %add_convert_fusion.7), channel_id=1, source_target_pairs={{0,96},{32,0},{64,32},{96,64},{1,97},{33,1},{65,33},{97,65},{2,98}... | collective-permute-start | bytes 405512 | tf_op jit(solution)/shard_map/ppermute | solution.py:24
  304.3 19.4 %collective-permute-start.48 = (bf16[104,704]{1,0:T(8,128)(2,1)S(1)}, bf16[104,704]{1,0:T(8,128)(2,1)S(1)}, u32[]{:S(2)}, u32[]{:S(2)}) collective-permute-start(bf16[104,704]{1,0:T(8,128)(2,1)S(1)} %add_convert_fusion.4), channel_id=1, source_target_pairs={{0,32},{32,64},{64,96},{96,0},{1,33},{33,65},{65,97},{97,1},{2,34}... | collective-permute-start | bytes 439304 | tf_op jit(solution)/shard_map/ppermute | solution.py:24
  304.6 17.4 %collective-permute-start.27 = (bf16[200,896]{1,0:T(8,128)(2,1)S(1)}, bf16[200,896]{1,0:T(8,128)(2,1)S(1)}, u32[]{:S(2)}, u32[]{:S(2)}) collective-permute-start(bf16[200,896]{1,0:T(8,128)(2,1)S(1)} %get-tuple-element.41), channel_id=1, source_target_pairs={{0,32},{32,64},{64,96},{96,0},{1,33},{33,65},{65,97},{97,1},{2,34}... | collective-permute-start | bytes 1075208 | tf_op jit(solution)/shard_map/ppermute | solution.py:24
  312.4 15.0 %collective-permute-start.40 = (bf16[200,896]{1,0:T(8,128)(2,1)S(1)}, bf16[200,896]{1,0:T(8,128)(2,1)S(1)}, u32[]{:S(2)}, u32[]{:S(2)}) collective-permute-start(bf16[200,896]{1,0:T(8,128)(2,1)S(1)} %get-tuple-element.35), channel_id=1, source_target_pairs={{0,32},{32,64},{64,96},{96,0},{1,33},{33,65},{65,97},{97,1},{2,34}... | collective-permute-start | bytes 1075208 | tf_op jit(solution)/shard_map/ppermute | solution.py:24
  313.3 14.0 %collective-permute-start.41 = (bf16[200,896]{1,0:T(8,128)(2,1)S(1)}, bf16[200,896]{1,0:T(8,128)(2,1)S(1)}, u32[]{:S(2)}, u32[]{:S(2)}) collective-permute-start(bf16[200,896]{1,0:T(8,128)(2,1)S(1)} %get-tuple-element.34), channel_id=1, source_target_pairs={{0,96},{32,0},{64,32},{96,64},{1,97},{33,1},{65,33},{97,65},{2,98}... | collective-permute-start | bytes 1075208 | tf_op jit(solution)/shard_map/ppermute | solution.py:24
  (41 other events, 425.1 us)
